TPU v7x, 128 devices: a whole 4x4x4 slice. The times are simulated.
128 devices in a mesh: grp: 4 (over z), ep: 32 (over x, y, core).
Axes of the slice: x: 4, y: 4, z: 4, core: 2. Of those that a mesh axis runs over, the one named last changes fastest.
Arguments:
- attention: bfloat16 [16384, 1024], P(('grp', 'ep')), may hold values from -6 to 6
- residual: bfloat16 [16384, 1024], P(('grp', 'ep')), may hold values from -6 to 6
- out_proj: bfloat16 [1024, 1024], P(None, 'grp'), may hold values from -0.1875 to 0.1875
- pre_gain: float32 [1024], replicated, may hold values from 0.25 to 1.75
- post_gain: float32 [1024], replicated, may hold values from 0.25 to 1.75
- slot_gate_up: bfloat16 [32, 1024, 1024], P('ep'), may hold values from -0.1875 to 0.1875
- slot_down: bfloat16 [32, 512, 1024], P('ep'), may hold values from -0.25 to 0.25
- expert_ids: int32 [16384, 8], P(('grp', 'ep')), may hold values from 0 to 31, all different within a row
- copy_choice: int32 [16384, 8], P(('grp', 'ep')), may hold values from 0 to 3
- placement: int32 [32], replicated, may hold values from 0 to 31, each once
- request_age: int32 [16384], P(('grp', 'ep')), may hold values from 0 to 1048575
- decode_flag: int32 [16384], P(('grp', 'ep')), may hold values 0 or 1
- capacity: int32 [4, 32], replicated, may hold values from 4 to 8, as said below
- route_weight: float32 [16384, 8], P(('grp', 'ep')), may hold values from 0.05 to 1
Outputs:
- layer_out: bfloat16 [16384, 1024], P(('grp', 'ep'))
Inputs may be any that keep to these rules, and one draw needn't show every extreme that they name: At least one block has capacity 8. `expert_ids`: each row names 8 different experts. `placement`: each slot holds a different expert.
All inputs are finite; a program needn't handle non-finite values. No bound on the sum of `decode_flag` on one device may be relied on, other than what follows from the above.
Results may differ from a plain program's by a relative error of at most 0.01.
Values may be sent and summed in bfloat16 or wider, within the bound.
A program may use at most 64 MiB of HBM per device.

v0:
```python
import jax
import jax.numpy as jnp
from jax import lax
from jax.sharding import PartitionSpec as P


def rms_scale(values, gain):
    meansq = jnp.mean(values * values, axis=-1, keepdims=True)
    return values * lax.rsqrt(meansq + 1e-06) * gain


def on_device(
    attention,
    residual,
    out_proj,
    pre_gain,
    post_gain,
    slot_gate_up,
    slot_down,
    expert_ids,
    copy_choice,
    placement,
    request_age,
    decode_flag,
    capacity,
    route_weight,
):
    groups = lax.axis_size("grp")
    owners = lax.axis_size("ep")
    devices_all = groups * owners
    rows_here = attention.shape[0]
    features = attention.shape[1]
    picks_row = expert_ids.shape[1]
    cap_size = max(2, rows_here * picks_row // devices_all)
    columns = jnp.dot(
        lax.all_gather(attention, "grp", axis=0, tiled=True),
        out_proj,
        preferred_element_type=jnp.float32,
    )
    attn_proj = lax.all_to_all(columns, "grp", split_axis=0, concat_axis=1, tiled=True)
    hidden_state = (residual.astype(jnp.float32) + attn_proj).astype(jnp.bfloat16)
    normed = rms_scale(hidden_state.astype(jnp.float32), pre_gain).astype(jnp.bfloat16)
    experts_all = placement.shape[0]
    slot_table = jnp.arange(owners, dtype=jnp.int32)
    matches = (placement[None, :] == jnp.arange(experts_all, dtype=jnp.int32)[:, None]).astype(
        jnp.int32
    )
    slot_of = jnp.sum(slot_table[None, :] * matches, axis=1)
    expert_hits = (
        expert_ids[:, :, None] == jnp.arange(experts_all, dtype=jnp.int32)[None, None, :]
    ).astype(jnp.int32)
    target = copy_choice * owners + jnp.sum(expert_hits * slot_of[None, None, :], axis=2)
    priority = decode_flag * 1048576 + request_age
    order = jnp.arange(rows_here, dtype=jnp.int32)
    ahead_mask = (priority[None, :] > priority[:, None]) | (
        priority[None, :] == priority[:, None]
    ) & (order[None, :] < order[:, None])
    target_hits = jnp.sum(
        (target[:, :, None] == jnp.arange(devices_all, dtype=jnp.int32)[None, None, :]).astype(
            jnp.bfloat16
        ),
        axis=1,
    )
    counts = jnp.dot(
        ahead_mask.astype(jnp.bfloat16), target_hits, preferred_element_type=jnp.float32
    )
    position = jnp.take_along_axis(counts, target, axis=1).astype(jnp.int32)
    granted = jnp.take(capacity.reshape(-1), target)
    accepted = position < granted
    total_slots = devices_all * cap_size
    index = jnp.where(accepted, target * cap_size + position, total_slots)
    spread_rows = jnp.broadcast_to(normed[:, None, :], (rows_here, picks_row, features)).reshape(
        rows_here * picks_row, features
    )
    buffer = (
        jnp.zeros((total_slots, features), jnp.bfloat16)
        .at[index.reshape(-1)]
        .set(spread_rows, mode="drop")
    )
    gate_up_local = slot_gate_up[0]
    down_local = slot_down[0]
    hidden_units = down_local.shape[0]
    arrived = lax.all_to_all(
        buffer.reshape(devices_all, cap_size, features),
        ("grp", "ep"),
        split_axis=0,
        concat_axis=0,
        tiled=True,
    )
    flattened = arrived.reshape(-1, features)
    gate_up = jnp.dot(flattened, gate_up_local, preferred_element_type=jnp.float32)
    expert_hidden = (jax.nn.silu(gate_up[:, :hidden_units]) * gate_up[:, hidden_units:]).astype(
        jnp.bfloat16
    )
    produced = jnp.dot(expert_hidden, down_local, preferred_element_type=jnp.float32).astype(
        jnp.bfloat16
    )
    returned = lax.all_to_all(
        produced.reshape(arrived.shape), ("grp", "ep"), split_axis=0, concat_axis=0, tiled=True
    )
    flat_back = returned.reshape(total_slots, features)
    expert_out = flat_back[jnp.minimum(index, total_slots - 1)]
    weights_kept = jnp.where(accepted, route_weight, jnp.float32(0.0))
    mixture = jnp.einsum("rk,rkd->rd", weights_kept, expert_out, preferred_element_type=jnp.float32)
    return rms_scale(hidden_state.astype(jnp.float32) + mixture, post_gain).astype(jnp.bfloat16)


def solution(mesh):
    placed = (
        P(("grp", "ep"), None),
        P(("grp", "ep"), None),
        P(None, "grp"),
        P(),
        P(),
        P("ep", None, None),
        P("ep", None, None),
        P(("grp", "ep"), None),
        P(("grp", "ep"), None),
        P(),
        P(("grp", "ep")),
        P(("grp", "ep")),
        P(),
        P(("grp", "ep"), None),
    )
    return jax.shard_map(
        on_device, mesh=mesh, in_specs=placed, out_specs=P(("grp", "ep"), None), check_vma=False
    )
```

profile of v0, /device:TPU:1, one launch (start us, length us, event | category | flops | bytes accessed | tf_op | source)
XLA Modules:
  0.0 155.6 jit_solution(14246727109927637221)
XLA Ops:
  6.5 0.7 all-gather.2.cloned.1.call-update
  7.3 0.8 select_reduce_fusion.1
  8.0 0.8 select_reduce_fusion
  8.8 0.7 bitcast_or_fusion
  9.8 0.2 fusion.17
  10.1 0.7 multiply_add_fusion.1
  10.7 0.2 fusion.20
  10.9 6.8 %gather_fusion.2 = f32[1024]{0:T(1024)S(1)} fusion(f32[128,128]{1,0:T(8,128)S(1)} %fusion.20, s32[1024]{0:T(1024)S(1)} %reshape.110), kind=kCustom, calls=%fused_computation.2 | custom fusion | bytes 16384 | tf_op jit(solution)/shard_map/jit(take_along_axis)/gather | solution.py:67
  18.2 6.6 %gather_fusion = s32[1024]{0:T(1024)S(1)} fusion(s32[128]{0:T(128)S(1)} %reshape.87, s32[1024]{0:T(1024)S(1)} %broadcast_clamp_fusion.1), kind=kCustom, calls=%fused_computation | custom fusion | bytes 12288 | tf_op jit(solution)/shard_map/jit(_take)/gather | solution.py:68
  24.9 10.7 %all-gather.2.cloned.1.call-done = bf16[512,1024]{1,0:T(8,128)(2,1)} async-done(((bf16[128,1024]{1,0:T(8,128)(2,1)}), bf16[512,1024]{1,0:T(8,128)(2,1)}) %all-gather.2.cloned.1.call-update) | async-done | bytes 1048592 | tf_op jit(solution)/shard_map/all_gather | solution.py:36
  35.6 2.5 %fusion.27 = f32[512,256]{1,0:T(8,128)} fusion(bf16[512,1024]{1,0:T(8,128)(2,1)} %all-gather.2.cloned.1.call-done, bf16[1024,256]{1,0:T(8,128)(2,1)S(1)} %copy-done.1), kind=kOutput, calls=%fused_computation.57 | convolution fusion | flops 268435456 | bytes 2097152 | tf_op jit(solution)/shard_map/dot_general | solution.py:35
  38.1 3.6 %all-to-all-start = ((f32[4,128,256]{2,1,0:T(8,128)}), f32[4,128,256]{2,1,0:T(8,128)S(1)}, u32[]{:S(2)}, u32[]{:S(2)}) async-start(f32[4,128,256]{2,1,0:T(8,128)} %bitcast), calls=%async_computation | async-start | bytes 1048576 | tf_op jit(solution)/shard_map/all_to_all | solution.py:40
  41.9 7.3 %all-to-all-done = f32[4,128,256]{2,1,0:T(8,128)S(1)} async-done(((f32[4,128,256]{2,1,0:T(8,128)}), f32[4,128,256]{2,1,0:T(8,128)S(1)}, u32[]{:S(2)}, u32[]{:S(2)}) %all-to-all-start) | async-done | bytes 524320 | tf_op jit(solution)/shard_map/all_to_all | solution.py:40
  49.2 0.2 fusion.13
  49.6 6.8 %scatter_custom_fusion = bf16[1024,1024]{1,0:T(8,128)(2,1)} fusion(s32[1024]{0:T(1024)S(1)} %bitcast.43, bf16[128,1024]{1,0:T(8,128)(2,1)S(1)} %fusion.15, bf16[]{:T(256)} %constant.29.clone.1), kind=kCustom, calls=%fused_computation.11 | custom fusion | bytes 2359298 | tf_op jit(solution)/shard_map/scatter | solution.py:78
  56.4 40.3 %all_to_all.29 = bf16[128,8,1024]{2,1,0:T(8,128)(2,1)S(1)} all-to-all(bf16[128,8,1024]{2,1,0:T(8,128)(2,1)} %bitcast.40), channel_id=1, replica_groups=mesh['grp'=4,'ep'=32] {'grp','ep'}, dimensions={0} | all-to-all | bytes 4194304 | tf_op jit(solution)/shard_map/all_to_all | solution.py:83
  96.7 2.4 %fusion.3 = f32[1024,1024]{1,0:T(8,128)S(1)} fusion(bf16[1,1024,1024]{2,1,0:T(8,128)(2,1)S(1)} %copy-done, bf16[128,8,1024]{2,1,0:T(8,128)(2,1)S(1)} %all_to_all.29), kind=kOutput, calls=%fused_computation.8 | convolution fusion | flops 2147483648 | bytes 8388608 | tf_op jit(solution)/shard_map/dot_general | solution.py:91
  99.1 2.6 %convert_bitcast_fusion = bf16[128,8,1024]{2,1,0:T(8,128)(2,1)} fusion(f32[1024,1024]{1,0:T(8,128)S(1)} %fusion.3, bf16[1,512,1024]{2,1,0:T(8,128)(2,1)S(1)} %copy-done.7), kind=kOutput, calls=%fused_computation.13 | convolution fusion | flops 1077936128 | bytes 7340032 | tf_op jit(solution)/shard_map/dot_general | solution.py:95
  101.7 5.5 %all-to-all-start.2 = ((bf16[128,8,1024]{2,1,0:T(8,128)(2,1)}), bf16[128,8,1024]{2,1,0:T(8,128)(2,1)}, u32[]{:S(2)}, u32[]{:S(2)}) async-start(bf16[128,8,1024]{2,1,0:T(8,128)(2,1)} %convert_bitcast_fusion), calls=%async_computation.2 | async-start | bytes 4194304 | tf_op jit(solution)/shard_map/all_to_all | solution.py:98
  107.6 29.9 %all-to-all-done.2 = bf16[128,8,1024]{2,1,0:T(8,128)(2,1)} async-done(((bf16[128,8,1024]{2,1,0:T(8,128)(2,1)}), bf16[128,8,1024]{2,1,0:T(8,128)(2,1)}, u32[]{:S(2)}, u32[]{:S(2)}) %all-to-all-start.2) | async-done | bytes 2097184 | tf_op jit(solution)/shard_map/all_to_all | solution.py:98
  137.5 7.9 %gather_fusion.1 = bf16[1024,1024]{1,0:T(8,128)(2,1)} fusion(bf16[1024,1024]{1,0:T(8,128)(2,1)} %bitcast.11, s32[1024]{0:T(1024)S(1)} %broadcast_clamp_fusion), kind=kCustom, calls=%fused_computation.1 | custom fusion | bytes 4198400 | tf_op jit(solution)/shard_map/gather | solution.py:102
  145.5 2.3 %fusion.1 = f32[128,1,1024]{2,1,0:T(1,128)S(1)} fusion(bf16[128,8,1]{1,2,0:T(2,128)(2,1)S(1)} %copy.31, bf16[1024,1024]{1,0:T(8,128)(2,1)} %gather_fusion.1), kind=kOutput, calls=%fused_computation.6 | convolution fusion | flops 2097152 | bytes 2623488 | tf_op jit(solution)/shard_map/rk,rkd->rd/dot_general | solution.py:104
  147.8 0.2 multiply_reduce_fusion
  147.9 0.8 multiply_convert_fusion
  (42 shorter events, 1.6 us)
Async XLA Ops:
  6.5 90.2 %copy-start = (bf16[1,1024,1024]{2,1,0:T(8,128)(2,1)S(1)}, bf16[1,1024,1024]{2,1,0:T(8,128)(2,1)}, u32[]{:S(2)}) copy-start(bf16[1,1024,1024]{2,1,0:T(8,128)(2,1)} %param.19) | copy-start | bytes 6291460
  6.5 29.1 %all-gather.2.cloned.1.call-start = ((), (), s32[]{:S(2)}) async-start(), calls=%async_computation.3 | async-start | bytes 1310720 | tf_op jit(solution)/shard_map/all_gather | solution.py:36
  10.9 7.2 %copy-start.6 = (s32[4,32]{1,0:T(4,128)S(1)}, s32[4,32]{1,0:T(4,128)}, u32[]{:S(2)}) copy-start(s32[4,32]{1,0:T(4,128)} %param.26) | copy-start | bytes 1540
  18.2 17.4 %copy-start.1 = (bf16[1024,256]{1,0:T(8,128)(2,1)S(1)}, bf16[1024,256]{1,0:T(8,128)(2,1)}, u32[]{:S(2)}) copy-start(bf16[1024,256]{1,0:T(8,128)(2,1)} %param.16) | copy-start | bytes 1572868
  24.9 24.3 %copy-start.2 = (bf16[128,1024]{1,0:T(8,128)(2,1)S(1)}, bf16[128,1024]{1,0:T(8,128)(2,1)}, u32[]{:S(2)}) copy-start(bf16[128,1024]{1,0:T(8,128)(2,1)} %param.15) | copy-start | bytes 786436
  38.1 11.3 %copy-start.3 = (f32[1024]{0:T(1024)S(1)}, f32[1024]{0:T(1024)}, u32[]{:S(2)}) copy-start(f32[1024]{0:T(1024)} %param.17) | copy-start | bytes 12292
  38.1 11.1 %all-to-all-start = ((f32[4,128,256]{2,1,0:T(8,128)}), f32[4,128,256]{2,1,0:T(8,128)S(1)}, u32[]{:S(2)}, u32[]{:S(2)}) async-start(f32[4,128,256]{2,1,0:T(8,128)} %bitcast), calls=%async_computation | async-start | bytes 1048576 | tf_op jit(solution)/shard_map/all_to_all | solution.py:40
  96.7 2.4 %copy-start.7 = (bf16[1,512,1024]{2,1,0:T(8,128)(2,1)S(1)}, bf16[1,512,1024]{2,1,0:T(8,128)(2,1)}, u32[]{:S(2)}) copy-start(bf16[1,512,1024]{2,1,0:T(8,128)(2,1)} %param.20) | copy-start | bytes 3145732
  101.7 5.7 %copy-start.5 = (f32[128,8]{0,1:T(8,128)S(1)}, f32[128,8]{0,1:T(8,128)}, u32[]{:S(2)}) copy-start(f32[128,8]{0,1:T(8,128)} %param.27) | copy-start | bytes 12292
  101.7 35.9 %all-to-all-start.2 = ((bf16[128,8,1024]{2,1,0:T(8,128)(2,1)}), bf16[128,8,1024]{2,1,0:T(8,128)(2,1)}, u32[]{:S(2)}, u32[]{:S(2)}) async-start(bf16[128,8,1024]{2,1,0:T(8,128)(2,1)} %convert_bitcast_fusion), calls=%async_computation.2 | async-start | bytes 4194304 | tf_op jit(solution)/shard_map/all_to_all | solution.py:98
  145.5 2.5 %copy-start.4 = (f32[1024]{0:T(1024)S(1)}, f32[1024]{0:T(1024)}, u32[]{:S(2)}) copy-start(f32[1024]{0:T(1024)} %param.18) | copy-start | bytes 12292
Sparse Core Ops, SparseCore 0:
  9.0 26.5 all-gather.1
where the time goes:
time: 156 us
  waiting for transfers between devices  48.6 us (31%)
  blocking collectives  40.3 us (26%)
  local copies, waits for them, and re-layouts  29.5 us (19%)
  between operations  13.6 us (9%)
  matrix products  9.91 us (6%)
  starting transfers between devices  9.14 us (6%)
  other arithmetic  4.53 us (3%)
    all_to_all x1, blocking collectives, on_device(): lax.all_to_all(buffer.reshape(devices_all, cap_size, features), ('grp', '...  40.3 us
    all_to_all x1, waiting for transfers between devices, on_device(): lax.all_to_all(produced.reshape(arrived.shape), ('grp', 'ep'), split_axis...  29.9 us
    all_gather x1, waiting for transfers between devices, on_device(): lax.all_gather(attention, 'grp', axis=0, tiled=True)  10.7 us
    gather x1, local copies, waits for them, and re-layouts, on_device(): expert_out = flat_back[jnp.minimum(index, total_slots - 1)]  7.92 us
    all_to_all x1, waiting for transfers between devices, on_device(): lax.all_to_all(columns, 'grp', split_axis=0, concat_axis=1, tiled=True)  7.26 us
    gather x5, local copies, waits for them, and re-layouts, on_device(): position = jnp.take_along_axis(counts, target, axis=1).astype(jnp.int32)  7.12 us
    scatter x1, local copies, waits for them, and re-layouts, on_device(): buffer = jnp.zeros((total_slots, features), jnp.bfloat16).at[index.reshap...  6.83 us
    gather x3, local copies, waits for them, and re-layouts, on_device(): granted = jnp.take(capacity.reshape(-1), target)  6.7 us
  transfers between devices with their start and end apart: 3, of which 3 were waited for; matrix products, arithmetic and copies ran while one was open for 12% of the time, Pallas kernels for 0%

commit v1 on v0

v1 whole, which is shorter than its diff:
```python
import functools

import jax
import jax.numpy as jnp
from jax import lax
from jax.experimental import pallas as pl
from jax.experimental.pallas import tpu as pltpu
from jax.sharding import PartitionSpec as P

MESH = pl.DeviceIdType.MESH
BF = jnp.bfloat16
F32 = jnp.float32
FAR = (2, 1, 3)
NEAR = (1, 3, 2)


def dot(a, b):
    return jnp.dot(a, b, preferred_element_type=F32)


def kernel(
    att_h, res_h, wo_h, pre_h, post_h, gu_h, dn_h, ids_h, cc_h, place_h, age_h, flag_h, cap_h, rw_h,
    out_ref,
    att, res, pre, post, gu, dn, ids, cc, place, age, flag, cap, rw,
    wfull, proj, hid, src1, s1, mw_src, mw_rcv, sel, comb_w, comp, rec, ob, comb, part_src, part_rcv,
    in_sem, w_s, w_r, f_s, f_r, m_s, m_r, a_s, a_r, d_s, d_r, e_s, e_r, p_s, p_r,
):
    z = lax.axis_index("grp")
    e = lax.axis_index("ep")
    x, y, c = e // 8, (e // 2) % 4, e % 2

    def at(dx, dy, dz, dc):
        return ((z + dz) % 4, (((x + dx) % 4) * 4 + (y + dy) % 4) * 2 + (c + dc) % 2)

    def along(half, d, dc):
        return at(d, 0, 0, dc) if half == 0 else at(0, d, 0, dc)

    bar = pltpu.get_barrier_semaphore()
    greet = [(0, 0, 1, 0), (0, 0, 2, 0), (0, 0, 3, 0), (0, 0, 0, 1)]
    for d in (1, 2, 3):
        for dc in (0, 1):
            greet += [(d, 0, 0, dc), (0, d, 0, dc)]
    for off in greet:
        pl.semaphore_signal(bar, inc=1, device_id=at(*off), device_id_type=MESH)

    loads = []
    for i, (src, dst) in enumerate(
        (
            (ids_h, ids), (cc_h, cc), (place_h, place), (age_h, age), (flag_h, flag), (cap_h, cap), (rw_h, rw),
            (att_h, att), (wo_h, wfull.at[0]), (res_h, res), (pre_h, pre), (post_h, post), (gu_h, gu), (dn_h, dn),
        )
    ):
        cp = pltpu.make_async_copy(src, dst, in_sem.at[i])
        cp.start()
        loads.append(cp)

    sends = []

    def remote(src, dst, ss, rs, dev):
        cp = pltpu.make_async_remote_copy(
            src_ref=src, dst_ref=dst, send_sem=ss, recv_sem=rs, device_id=dev, device_id_type=MESH
        )
        cp.start()
        sends.append(cp)
        return cp

    pl.semaphore_wait(bar, len(greet))
    w_cp = {}
    for d in NEAR:
        w_cp[d] = remote(wo_h.at[c], wfull.at[d, c], w_s.at[d - 1], w_r.at[d - 1], at(0, 0, d, 0))

    for cp in loads[:7]:
        cp.wait()
    row = lax.broadcasted_iota(jnp.int32, (128, 128), 0)
    lane = lax.broadcasted_iota(jnp.int32, (128, 128), 1)
    pr_row = (flag[...] * 1048576 + age[...]).astype(F32)
    pr_col = jnp.sum(jnp.where(row == lane, jnp.broadcast_to(pr_row, (128, 128)), 0.0), axis=1, keepdims=True)
    ahead = jnp.where((pr_col > pr_row) | ((pr_col == pr_row) & (row < lane)), 1.0, 0.0)
    t = lax.broadcasted_iota(jnp.int32, (128, 32), 0)
    slot_lane = lax.broadcasted_iota(jnp.int32, (128, 32), 1)
    copy_of = t % 4
    slot = (((x + t // 32) % 4) * 4 + (y + (t // 4) % 4) % 4) * 2 + (c + (t // 16) % 2) % 2
    here = slot_lane == slot
    expert = jnp.sum(jnp.where(here, place[...].astype(F32), 0.0), axis=1, keepdims=True)
    code_col = expert * 4.0 + copy_of[:, :1].astype(F32)
    capf = cap[...].astype(F32)
    cap_sel = jnp.zeros((128, 32), F32)
    for g in range(4):
        cap_sel = jnp.where(here & (copy_of == g), capf[g : g + 1, :], cap_sel)
    cap_col = jnp.sum(cap_sel, axis=1, keepdims=True)
    code = (ids[...] * 4 + cc[...]).astype(F32)
    hits = jnp.zeros((128, 128), F32)
    weight = jnp.zeros((128, 128), F32)
    for k in range(8):
        same = code_col == code[k : k + 1, :]
        hits = jnp.where(same, 1.0, hits)
        weight = jnp.where(same, rw[k : k + 1, :], weight)
    counts = dot(hits.astype(BF), ahead.astype(BF))
    place_in = jnp.where((hits > 0.5) & (counts < cap_col), counts, 99.0)
    mw = jnp.concatenate([place_in, weight], axis=1).astype(BF)
    pw = jnp.concatenate([place_in, weight], axis=1)
    for d in range(4):
        mw_src[0, d] = pw[d * 32 : d * 32 + 32].astype(BF)
        blocks = []
        for dc in range(2):
            for dx in range(4):
                lo = dx * 32 + dc * 16 + d * 4
                blocks.append(pw[lo : lo + 4])
        mw_src[1, d] = jnp.concatenate(blocks, axis=0).astype(BF)
    del mw
    m_cp = {}
    for d in NEAR:
        for h in (0, 1):
            m_cp[h, d] = remote(
                mw_src.at[h, d], mw_rcv.at[h, d - 1], m_s.at[h, d - 1], m_r.at[h, d - 1], along(h, d, 0)
            )

    grow = jnp.where(
        lax.broadcasted_iota(jnp.int32, (256, 32), 0) // 8 == lax.broadcasted_iota(jnp.int32, (256, 32), 1), 1.0, 0.0
    ).astype(BF)
    p_row = (lax.broadcasted_iota(jnp.int32, (256, 128), 0) % 8).astype(F32)
    p_lane = (lax.broadcasted_iota(jnp.int32, (128, 256), 1) % 8).astype(F32)

    def expand(h, d, ref):
        both = ref[...]
        sel[h, d] = jnp.where(dot(grow, both[:, :128]) == p_row, 1.0, 0.0).astype(BF)
        wide = lax.dot_general(both, grow, (((0,), (1,)), ((), ())), preferred_element_type=F32)
        comb_w[h, d] = jnp.where(wide[:128] == p_lane, wide[128:], 0.0).astype(BF)

    for h in (0, 1):
        expand(h, 0, mw_src.at[h, 0])

    loads[7].wait()
    loads[8].wait()

    def project(d):
        proj[(z - d) % 4] = dot(att[...], wfull[d].reshape(1024, 256))

    project(0)
    f_cp = {}
    for d in NEAR:
        w_cp[d].wait_recv()
        f_cp[d] = remote(wfull.at[d, c], wfull.at[d, c], f_s.at[d - 1], f_r.at[d - 1], at(0, 0, 0, 1))
        if d == 1:
            for dd in NEAR:
                for h in (0, 1):
                    m_cp[h, dd].wait_recv()
                    expand(h, dd, mw_rcv.at[h, dd - 1])
        if d == 3:
            f_cp[1].wait_recv()
            project(1)
    f_cp[3].wait_recv()
    project(3)
    f_cp[2].wait_recv()
    project(2)

    for cp in loads[9:12]:
        cp.wait()
    total = jnp.zeros((128, 1), F32)
    for q in range(4):
        cols = slice(q * 256, q * 256 + 256)
        part = (res[:, cols].astype(F32) + proj[q]).astype(BF)
        hid[:, cols] = part
        wide = part.astype(F32)
        total = total + jnp.sum(wide * wide, axis=1, keepdims=True)
    scale = lax.rsqrt(total * (1.0 / 1024.0) + 1e-06)
    for q in range(4):
        cols = slice(q * 256, q * 256 + 256)
        src1[q // 2, :, (q % 2) * 256 : (q % 2) * 256 + 256] = (
            hid[:, cols].astype(F32) * scale * pre[:, cols]
        ).astype(BF)

    a_cp = {}
    for d in FAR:
        for h in (0, 1):
            a_cp[h, d] = remote(src1.at[h], s1.at[h, d - 1], a_s.at[h, d - 1], a_r.at[h, d - 1], along(h, d, 0))

    def compact(h, d, rows):
        comp[h, :, d] = dot(sel[h, d], rows[...]).astype(BF).reshape(8, 32, 512)

    for h in (0, 1):
        compact(h, 0, src1.at[h])
    for d in NEAR:
        for h in (0, 1):
            a_cp[h, d].wait_recv()
            compact(h, d, s1.at[h, d - 1])

    d_cp = {}
    for dc in (0, 1):
        for d in FAR if dc == 0 else FAR + (0,):
            for h in (0, 1):
                i = dc * 4 + d
                d_cp[h, i] = remote(
                    comp.at[h, i], rec.at[h, i], d_s.at[h, i - 1], d_r.at[h, i - 1], along(1 - h, d, dc)
                )

    loads[12].wait()
    loads[13].wait()
    e_cp = {}
    for dc in (0, 1):
        for d in range(4):
            for h in (0, 1):
                if dc * 4 + d:
                    d_cp[h, dc * 4 + d].wait_recv()

        def got(h, i):
            return comp[h, 0] if i == 0 else rec[h, i]

        for pair in (0, 1):
            xa, xb = [], []
            for dy in (2 * pair, 2 * pair + 1):
                xa.append(got(0, dc * 4 + dy).reshape(128, 512))
                for dx in range(4):
                    xb.append(comp[1, 0, dy] if dc * 4 + dx == 0 else rec[1, dc * 4 + dx, dy])
            xa = jnp.concatenate(xa, axis=0)
            xb = jnp.concatenate(xb, axis=0)
            gate = dot(xa, gu[:512, :512]) + dot(xb, gu[512:, :512])
            up = dot(xa, gu[:512, 512:]) + dot(xb, gu[512:, 512:])
            inner = (gate / (1.0 + jnp.exp(-gate)) * up).astype(BF)
            made = dot(inner, dn[...]).astype(BF)
            for k in (0, 1):
                dy = 2 * pair + k
                ob[0, dc * 4 + dy] = made[k * 128 : k * 128 + 128, :512].reshape(4, 32, 512)
                for dx in range(4):
                    ob[1, dc * 4 + dx, dy] = made[k * 128 + dx * 32 : k * 128 + dx * 32 + 32, 512:]
        for d in FAR if dc == 0 else FAR + (0,):
            for h in (0, 1):
                i = dc * 4 + d
                e_cp[h, i] = remote(
                    ob.at[h, i], comb.at[h, i], e_s.at[h, i - 1], e_r.at[h, i - 1], along(1 - h, 4 - d, dc)
                )

    for dc in (0, 1):
        for d in range(4):
            for h in (0, 1):
                if dc * 4 + d:
                    e_cp[h, dc * 4 + d].wait_recv()

    def summed(h, d):
        back = jnp.concatenate([ob[h, 0, d]] + [comb[h, i, d] for i in range(1, 8)], axis=0)
        return dot(comb_w[h, d], back)

    p_cp = {}
    for d in FAR:
        for h in (0, 1):
            part_src[h, d - 1] = summed(h, d).astype(BF)
            p_cp[h, d] = remote(
                part_src.at[h, d - 1], part_rcv.at[h, d - 1], p_s.at[h, d - 1], p_r.at[h, d - 1], along(h, 4 - d, 0)
            )
    values = []
    total = jnp.zeros((128, 1), F32)
    for h in (0, 1):
        mix = summed(h, 0)
        for d in NEAR:
            p_cp[h, d].wait_recv()
            mix = mix + part_rcv[h, d - 1].astype(F32)
        v = hid[:, h * 512 : h * 512 + 512].astype(F32) + mix
        total = total + jnp.sum(v * v, axis=1, keepdims=True)
        values.append(v)
    scale = lax.rsqrt(total * (1.0 / 1024.0) + 1e-06)
    for h in (0, 1):
        cols = slice(h * 512, h * 512 + 512)
        out_ref[:, cols] = (values[h] * scale * post[:, cols]).astype(BF)
    for cp in sends:
        cp.wait_send()


def on_device(
    attention, residual, out_proj, pre_gain, post_gain, slot_gate_up, slot_down, expert_ids, copy_choice,
    placement, request_age, decode_flag, capacity, route_weight,
):
    dma = pltpu.SemaphoreType.DMA
    vm = pltpu.VMEM
    return pl.pallas_call(
        kernel,
        out_shape=jax.ShapeDtypeStruct((128, 1024), BF),
        in_specs=[pl.BlockSpec(memory_space=pl.ANY)] * 14,
        out_specs=pl.BlockSpec(memory_space=pltpu.VMEM),
        scratch_shapes=[
            vm((128, 1024), BF), vm((128, 1024), BF), vm((1, 1024), F32), vm((1, 1024), F32),
            vm((1024, 1024), BF), vm((512, 1024), BF),
            vm((8, 128), jnp.int32), vm((8, 128), jnp.int32), vm((1, 32), jnp.int32),
            vm((1, 128), jnp.int32), vm((1, 128), jnp.int32), vm((4, 32), jnp.int32), vm((8, 128), F32),
            vm((4, 2, 512, 256), BF), vm((4, 128, 256), F32), vm((128, 1024), BF),
            vm((2, 128, 512), BF), vm((2, 3, 128, 512), BF),
            vm((2, 4, 32, 256), BF), vm((2, 3, 32, 256), BF),
            vm((2, 4, 256, 128), BF), vm((2, 4, 128, 256), BF),
            vm((2, 8, 4, 32, 512), BF), vm((2, 8, 4, 32, 512), BF),
            vm((2, 8, 4, 32, 512), BF), vm((2, 8, 4, 32, 512), BF),
            vm((2, 3, 128, 512), BF), vm((2, 3, 128, 512), BF),
            dma((14,)),
            dma((3,)), dma((3,)), dma((3,)), dma((3,)),
            dma((2, 3)), dma((2, 3)), dma((2, 3)), dma((2, 3)),
            dma((2, 7)), dma((2, 7)), dma((2, 7)), dma((2, 7)),
            dma((2, 3)), dma((2, 3)),
        ],
        compiler_params=pltpu.CompilerParams(
            collective_id=0, has_side_effects=True, vmem_limit_bytes=67_000_000
        ),
        cost_estimate=pl.CostEstimate(flops=4_000_000_000, bytes_accessed=5_000_000, transcendentals=600_000),
        name="moe_layer",
    )(
        attention, residual, out_proj.reshape(2, 512, 256), pre_gain.reshape(1, -1), post_gain.reshape(1, -1),
        slot_gate_up[0], slot_down[0], expert_ids.T, copy_choice.T, placement.reshape(1, -1),
        request_age.reshape(1, -1), decode_flag.reshape(1, -1), capacity, route_weight.T,
    )


def solution(mesh):
    rows = P(("grp", "ep"), None)
    placed = (
        rows, rows, P(None, "grp"), P(), P(), P("ep", None, None), P("ep", None, None), rows, rows, P(),
        P(("grp", "ep")), P(("grp", "ep")), P(), rows,
    )
    return jax.shard_map(on_device, mesh=mesh, in_specs=placed, out_specs=rows, check_vma=False)
```

time: 156 us -> 72.1 us (0.46)
  Pallas kernels: 0 us -> 70.3 us
  waiting for transfers between devices: 48.6 us -> 0 us
  blocking collectives: 40.3 us -> 0 us
  local copies, waits for them, and re-layouts: 29.5 us -> 1.67 us
  between operations: 13.6 us -> 0.01 us
  matrix products: 9.91 us -> 0 us
  starting transfers between devices: 9.14 us -> 0 us
  other arithmetic: 4.53 us -> 0 us
    pallas_call x0 -> x1, Pallas kernels: none -> 70.3 us  [on_device(): pl.pallas_call(kernel, out_shape=jax.ShapeDtypeStruct((128, 1024), BF), i...]
    all_to_all x1 -> x0, blocking collectives: 40.3 us -> none  [on_device(): lax.all_to_all(buffer.reshape(devices_all, cap_size, features), ('grp', '...]
    all_to_all x2 -> x0, waiting for transfers between devices: 37.2 us -> none  [the longest x1 29.9 us: on_device(): lax.all_to_all(produced.reshape(arrived.shape), ('grp', 'ep'), split_axis...]
    gather x9 -> x0, local copies, waits for them, and re-layouts: 21.7 us -> none  [the longest x1 7.92 us: on_device(): expert_out = flat_back[jnp.minimum(index, total_slots - 1)]]
    all_gather x1 -> x0, waiting for transfers between devices: 10.7 us -> none  [on_device(): lax.all_gather(attention, 'grp', axis=0, tiled=True)]
    dot_general x5 -> x0, matrix products: 9.91 us -> none  [the longest x1 2.6 us: on_device(): jnp.dot(expert_hidden, down_local, preferred_element_type=jnp.float32)]
    all_to_all x2 -> x0, starting transfers between devices: 9.14 us -> none  [the longest x1 5.54 us: on_device(): lax.all_to_all(produced.reshape(arrived.shape), ('grp', 'ep'), split_axis...]
    scatter x1 -> x0, local copies, waits for them, and re-layouts: 6.83 us -> none  [on_device(): buffer = jnp.zeros((total_slots, features), jnp.bfloat16).at[index.reshap...]
  transfers between devices with their start and end apart: 3 -> 0, of which waited for: 3 -> 0; matrix products, arithmetic and copies ran while one was open for 12% -> 0% of each run, Pallas kernels for 0% -> 0%
where the time goes in v1:
time: 72.1 us; the launch traced here: 72 us
  Pallas kernels  70.3 us (98%)
  local copies, waits for them, and re-layouts  1.67 us (2%)
    pallas_call x1, Pallas kernels, on_device(): pl.pallas_call(kernel, out_shape=jax.ShapeDtypeStruct((128, 1024), BF), i...  70.3 us
    unnamed x1, local copies, waits for them, and re-layouts  1.67 us

profile of v1, /device:TPU:1, one launch (start us, length us, event | category | flops | bytes accessed | tf_op | source)
XLA Modules:
  0.0 72.0 jit_solution(2003685210774387469)
XLA Ops:
  0.0 70.3 %moe_layer.1 = bf16[128,1024]{1,0:T(8,128)(2,1)} custom-call(bf16[128,1024]{1,0:T(8,128)(2,1)} %att_h.1, bf16[128,1024]{1,0:T(8,128)(2,1)} %res_h.1, bf16[2,512,256]{2,1,0:T(8,128)(2,1)} %bitcast.13, f32[1,1024]{1,0:T(1,128)} %bitcast.14, f32[1,1024]{1,0:T(1,128)} %bitcast.15, bf16[1024,1024]{1,0:T(8,128)(2,1)} %bitcast.11, bf16[512,1024]{1,0:T(8,128)(2,1)} %bitcast.12, ...), custom_call_target="tpu_custom_call" | custom-call | flops 4000000000 | bytes 5000000 | tf_op jit(solution)/shard_map/moe_layer/pallas_call | solution.py:274
  70.3 1.7 %copy.16 = bf16[128,1024]{1,0:T(8,128)(2,1)} copy(bf16[128,1024]{1,0:T(8,128)(2,1)} %moe_layer.1) | data formatting | bytes 524288

commit v2 on v1

v2 whole, which is shorter than its diff:
```python
import jax
import jax.numpy as jnp
from jax import lax
from jax.experimental import pallas as pl
from jax.experimental.pallas import tpu as pltpu
from jax.sharding import PartitionSpec as P

MESH = pl.DeviceIdType.MESH
BF = jnp.bfloat16
F32 = jnp.float32
DIST = (0, 1, 3, 2)


def dot(a, b):
    return jnp.dot(a, b, preferred_element_type=F32)


def kernel(
    att_h, res_h, wo_h, pre_h, post_h, gu_h, dn_h, ids_h, cc_h, place_h, age_h, flag_h, cap_h, rw_h,
    out_ref,
    pre, post, gu, dn, ids, cc, place, age, flag, cap, rw,
    att, res, wmine, hall, hfin, mw_src, mw_all, sel, comb_w, ss_src, ss_rcv,
    comp, comp2, rec, rec2, ob, comb, part_src, part_rcv,
    in_sem, loc_sem, w_s, w_r, a_s, a_r, r_s, r_r, m_s, m_r, h_s, h_r, q_s, q_r, d_s, d_r, e_s, e_r, p_s, p_r,
):
    z = lax.axis_index("grp")
    e = lax.axis_index("ep")
    x, y, c = e // 8, (e // 2) % 4, e % 2
    other = 1 - c

    def dev(dx, dy, core):
        return (z, (((x + dx) % 4) * 4 + (y + dy) % 4) * 2 + core)

    def first(d, core):
        return dev(d * other, d * c, core)

    def second(d, core):
        return dev(d * c, d * other, core)

    bar = pltpu.get_barrier_semaphore()
    greet = [((z + d) % 4, e) for d in (1, 2, 3)] + [dev(0, 0, other)]
    for d in (1, 2, 3):
        for core in (0, 1):
            greet += [dev(d, 0, core), dev(0, d, core)]
    for to in greet:
        pl.semaphore_signal(bar, inc=1, device_id=to, device_id_type=MESH)

    def half_of(half):
        return pl.ds(pl.multiple_of(half * 512, 512), 512)

    loads = []
    for i, (src, dst) in enumerate(
        (
            (ids_h, ids), (cc_h, cc), (place_h, place), (age_h, age), (flag_h, flag), (cap_h, cap), (rw_h, rw),
            (att_h, att.at[0, c]), (res_h.at[:, half_of(c)], res.at[0, c]), (pre_h, pre), (post_h, post),
            (gu_h, gu), (dn_h, dn),
        )
    ):
        cp = pltpu.make_async_copy(src, dst, in_sem.at[i])
        cp.start()
        loads.append(cp)
    has_w = c == z // 2
    w_local = pltpu.make_async_copy(wo_h, wmine.at[z % 2], in_sem.at[13])

    sends = []

    def remote(src, dst, ss, rs, to):
        cp = pltpu.make_async_remote_copy(
            src_ref=src, dst_ref=dst, send_sem=ss, recv_sem=rs, device_id=to, device_id_type=MESH
        )
        cp.start()
        sends.append(cp)

    def arrived(dst, rs):
        pltpu.make_async_remote_copy(
            src_ref=dst, dst_ref=dst, send_sem=rs, recv_sem=rs, device_id=dev(0, 0, other), device_id_type=MESH
        ).wait_recv()

    w_cp = [
        pltpu.make_async_remote_copy(
            src_ref=wo_h, dst_ref=wmine.at[z % 2], send_sem=w_s.at[d - 1], recv_sem=w_r.at[z % 2],
            device_id=((z + d) % 4, e), device_id_type=MESH,
        )
        for d in (2, 1, 3)
    ]
    pl.semaphore_wait(bar, len(greet))

    @pl.when(has_w)
    def _():
        w_local.start()
        for cp in w_cp:
            cp.start()

    k = 0
    for p in (1, 2):
        d = DIST[p]
        for half, to in ((0, dev(d, 0, 0)), (1, dev(0, d, 1))):
            remote(att_h, att.at[p, c], a_s.at[k], a_r.at[p, c], to)
            remote(res_h.at[:, half * 512 : half * 512 + 512], res.at[p, c], r_s.at[k], r_r.at[p, c], to)
            k += 1
    remote(att_h, att.at[0, c], a_s.at[k], a_r.at[0, c], dev(0, 0, other))
    remote(res_h.at[:, half_of(other)], res.at[0, c], r_s.at[k], r_r.at[0, c], dev(0, 0, other))

    for cp in loads[:7]:
        cp.wait()
    row = lax.broadcasted_iota(jnp.int32, (128, 128), 0)
    lane = lax.broadcasted_iota(jnp.int32, (128, 128), 1)
    eye = row == lane
    pr_row = (flag[...] * 1048576 + age[...]).astype(F32)
    pr_col = jnp.sum(jnp.where(eye, pr_row, 0.0), axis=1, keepdims=True)
    ahead = jnp.where((pr_col > pr_row) | ((pr_col == pr_row) & (row < lane)), 1.0, 0.0)
    t = lax.broadcasted_iota(jnp.int32, (128, 32), 0)
    slot_lane = lax.broadcasted_iota(jnp.int32, (128, 32), 1)
    copy_of = t % 4
    px, py = t // 32, (t // 4) % 4
    dx = jnp.where(px < 2, px, 5 - px)
    dy = jnp.where(py < 2, py, 5 - py)
    slot = (((x + dx) % 4) * 4 + (y + dy) % 4) * 2 + (t // 16) % 2
    here = slot_lane == slot
    expert = jnp.sum(jnp.where(here, place[...].astype(F32), 0.0), axis=1, keepdims=True)
    code_col = expert * 4.0 + copy_of[:, :1].astype(F32)
    capf = cap[...].astype(F32)
    cap_sel = jnp.zeros((128, 32), F32)
    for g in range(4):
        cap_sel = jnp.where(here & (copy_of == g), capf[g : g + 1, :], cap_sel)
    cap_col = jnp.sum(cap_sel, axis=1, keepdims=True)
    code = (ids[...] * 4 + cc[...]).astype(F32)
    hits = jnp.zeros((128, 128), F32)
    weight = jnp.zeros((128, 128), F32)
    for i in range(8):
        same = code_col == code[i : i + 1, :]
        hits = jnp.where(same, 1.0, hits)
        weight = jnp.where(same, rw[i : i + 1, :], weight)
    counts = dot(hits.astype(BF), ahead.astype(BF))
    place_in = jnp.where((hits > 0.5) & (counts < cap_col), counts, 99.0)
    pw = jnp.concatenate([place_in, weight], axis=1)
    for p in range(4):
        mw_src[0, p] = pw[p * 32 : p * 32 + 32].astype(BF)
        blocks = []
        for core in range(2):
            for q in range(4):
                lo = q * 32 + core * 16 + p * 4
                blocks.append(pw[lo : lo + 4])
        mw_src[1, p] = jnp.concatenate(blocks, axis=0).astype(BF)
    k = 0
    for p in (1, 2, 3):
        d = DIST[p]
        for half, to in ((0, dev(d, 0, 0)), (1, dev(0, d, 1))):
            remote(mw_src.at[half, p], mw_all.at[p, c], m_s.at[k], m_r.at[p, c], to)
            k += 1
    remote(mw_src.at[other, 0], mw_all.at[0, c], m_s.at[k], m_r.at[0, c], dev(0, 0, other))
    mw_all[0, c] = mw_src[c, 0]

    grow = jnp.where(
        lax.broadcasted_iota(jnp.int32, (256, 32), 0) // 8 == lax.broadcasted_iota(jnp.int32, (256, 32), 1), 1.0, 0.0
    ).astype(BF)
    p_row = (lax.broadcasted_iota(jnp.int32, (256, 128), 0) % 8).astype(F32)
    p_lane = (lax.broadcasted_iota(jnp.int32, (128, 256), 1) % 8).astype(F32)
    arrived(mw_all.at[0, other], m_r.at[0, other])
    for p in range(4):
        for core in (0, 1):
            if p:
                arrived(mw_all.at[p, core], m_r.at[p, core])
            both = mw_all[p, core]
            sel[p, core] = jnp.where(dot(grow, both[:, :128]) == p_row, 1.0, 0.0).astype(BF)
            wide = lax.dot_general(both, grow, (((0,), (1,)), ((), ())), preferred_element_type=F32)
            comb_w[p, core] = jnp.where(wide[:128] == p_lane, wide[128:], 0.0).astype(BF)

    for cp in loads[7:]:
        cp.wait()
    arrived(att.at[0, other], a_r.at[0, other])
    arrived(res.at[0, other], r_r.at[0, other])

    @pl.when(has_w)
    def _():
        w_local.wait()

    for q in (0, 1):

        @pl.when(c * 2 + q != z)
        def _():
            arrived(wmine.at[q], w_r.at[q])

    def project(p):
        rows = att[p].reshape(256, 1024)
        for q in (0, 1):
            cols = slice(q * 256, q * 256 + 256)
            part = dot(rows, wmine[q]).reshape(2, 128, 256)
            hall[p, :, :, cols] = (res[p, :, :, cols].astype(F32) + part).astype(BF)

    def squares(p, core):
        wide = hall[p, core].astype(F32)
        return jnp.sum(wide * wide, axis=1, keepdims=True)

    project(0)
    remote(hall.at[0], hall.at[3], h_s.at[0], h_r.at[0], first(2, c))
    remote(hall.at[0, other], hfin.at[c], h_s.at[1], h_r.at[1], dev(0, 0, other))
    own_ss = {}
    for core in (0, 1):
        own_ss[0, core] = squares(0, core)
        ss_src[core : core + 1, :] = jnp.sum(jnp.where(eye, own_ss[0, core], 0.0), axis=0, keepdims=True)
    remote(ss_src, ss_rcv.at[0], q_s.at[0], q_r.at[0], dev(0, 0, other))
    for p in (1, 2, 3):
        remote(ss_src, ss_rcv.at[p], q_s.at[p], q_r.at[p], second(DIST[p], other))
    hfin[c] = hall[0, c]
    for p in (1, 2):
        for core in (0, 1):
            arrived(att.at[p, core], a_r.at[p, core])
            arrived(res.at[p, core], r_r.at[p, core])
        project(p)
        for core in (0, 1):
            own_ss[p, core] = squares(p, core)

    gain = pre[c]

    def compact(p, core):
        total = own_ss[p, core] + jnp.sum(jnp.where(eye, ss_rcv[p, core : core + 1, :], 0.0), axis=1, keepdims=True)
        scale = lax.rsqrt(total * (1.0 / 1024.0) + 1e-06)
        normed = (hall[p, core].astype(F32) * scale * gain).astype(BF)
        return dot(sel[p, core], normed).astype(BF).reshape(2, 4, 32, 512)

    local = []

    def spread(src, dst, kind):
        for p in (3, 1, 2):
            for core in (0, 1):
                remote(
                    src.at[core, p], dst(p), d_s.at[kind, core * 3 + p - 1], d_r.at[kind, c * 3 + p - 1],
                    second(DIST[p], core),
                )
        remote(src.at[other, 0], dst(0), d_s.at[kind, 6], d_r.at[kind, 6], dev(0, 0, other))
        cp = pltpu.make_async_copy(src.at[c, 0], dst(0), loc_sem.at[kind])
        cp.start()
        local.append(cp)

    for p in range(3):
        arrived(ss_rcv.at[p], q_r.at[p])
        comp[0, :, :, p] = compact(p, 0)
    spread(comp.at[0], lambda p: rec.at[c, p, 0], 0)
    arrived(hall.at[3], h_r.at[0])
    arrived(ss_rcv.at[3], q_r.at[3])
    for core in (0, 1):
        own_ss[3, core] = squares(3, core)
        comp2[:, :, core] = compact(3, core)
    spread(comp2, lambda p: rec2.at[c, p], 1)
    for p in range(3):
        comp[1, :, :, p] = compact(p, 1)
    spread(comp.at[1], lambda p: rec.at[c, p, 1], 2)

    def places_in(src, kind):
        for half in (0, 1):
            for p in (1, 2, 3):
                arrived(src(half, p), d_r.at[kind, half * 3 + p - 1])
        arrived(src(other, 0), d_r.at[kind, 6])
        local[kind].wait()

    back = []
    for rows_of in (0, 1):
        if rows_of == 0:
            places_in(lambda half, p: rec.at[half, p, 0], 0)
            places_in(lambda half, p: rec2.at[half, p], 1)
        else:
            places_in(lambda half, p: rec.at[half, p, 1], 2)

        def got(half, p, q):
            return rec2[half, p, rows_of] if q == 3 else rec[half, p, rows_of, q]

        for pair in (0, 1):
            blocks = [(qy, qx) for qy in (2 * pair, 2 * pair + 1) for qx in range(4)]
            xa = jnp.concatenate([got(0, qy, qx) for qy, qx in blocks], axis=0)
            xb = jnp.concatenate([got(1, qx, qy) for qy, qx in blocks], axis=0)
            gate = dot(xa, gu[:512, :512]) + dot(xb, gu[512:, :512])
            up = dot(xa, gu[:512, 512:]) + dot(xb, gu[512:, 512:])
            inner = (gate / (1.0 + jnp.exp(-gate)) * up).astype(BF)
            made = dot(inner, dn[...]).astype(BF)
            for i, (qy, qx) in enumerate(blocks):
                ob[0, qy, rows_of, qx] = made[i * 32 : i * 32 + 32, :512]
                ob[1, qx, rows_of, qy] = made[i * 32 : i * 32 + 32, 512:]
        for p in (3, 1, 2):
            d = 4 - DIST[p]
            for half, to in ((0, dev(0, d, 0)), (1, dev(d, 0, 1))):
                remote(
                    ob.at[half, p, rows_of], comb.at[p, c, rows_of], e_s.at[rows_of, half * 3 + p - 1],
                    e_r.at[rows_of, c * 3 + p - 1], to,
                )
        remote(
            ob.at[other, 0, rows_of], comb.at[0, c, rows_of], e_s.at[rows_of, 6], e_r.at[rows_of, 6], dev(0, 0, other)
        )
        cp = pltpu.make_async_copy(ob.at[c, 0, rows_of], comb.at[0, c, rows_of], loc_sem.at[3 + rows_of])
        cp.start()
        back.append(cp)

    for rows_of in (0, 1):
        for core in (0, 1):
            for p in (1, 2, 3):
                arrived(comb.at[p, core, rows_of], e_r.at[rows_of, core * 3 + p - 1])
        arrived(comb.at[0, other, rows_of], e_r.at[rows_of, 6])
        back[rows_of].wait()
        for p in (3, 1, 2, 0):
            rows = jnp.concatenate([comb[q, core, rows_of, p] for core in (0, 1) for q in range(4)], axis=0)
            part_src[p, rows_of] = dot(comb_w[p, rows_of], rows).astype(BF)
            if p:
                remote(
                    part_src.at[p, rows_of], part_rcv.at[c, p], p_s.at[rows_of * 3 + p - 1], p_r.at[c * 3 + p - 1],
                    first(4 - DIST[p], rows_of),
                )
    remote(part_src.at[0, other], part_rcv.at[c, 0], p_s.at[6], p_r.at[6], dev(0, 0, other))
    part_rcv[c, 0] = part_src[0, c]
    arrived(hfin.at[other], h_r.at[1])
    arrived(part_rcv.at[other, 0], p_r.at[6])
    values = []
    total = jnp.zeros((128, 1), F32)
    for half in (0, 1):
        v = hfin[half].astype(F32) + part_rcv[half, 0].astype(F32)
        for p in (1, 2, 3):
            arrived(part_rcv.at[half, p], p_r.at[half * 3 + p - 1])
            v = v + part_rcv[half, p].astype(F32)
        total = total + jnp.sum(v * v, axis=1, keepdims=True)
        values.append(v)
    scale = lax.rsqrt(total * (1.0 / 1024.0) + 1e-06)
    for half in (0, 1):
        cols = slice(half * 512, half * 512 + 512)
        out_ref[:, cols] = (values[half] * scale * post[:, cols]).astype(BF)
    for cp in sends:
        cp.wait_send()

    @pl.when(has_w)
    def _():
        for cp in w_cp:
            cp.wait_send()


def on_device(
    attention, residual, out_proj, pre_gain, post_gain, slot_gate_up, slot_down, expert_ids, copy_choice,
    placement, request_age, decode_flag, capacity, route_weight,
):
    dma = pltpu.SemaphoreType.DMA
    vm = pltpu.VMEM
    return pl.pallas_call(
        kernel,
        out_shape=jax.ShapeDtypeStruct((128, 1024), BF),
        in_specs=[pl.BlockSpec(memory_space=pl.ANY)] * 14,
        out_specs=pl.BlockSpec(memory_space=pltpu.VMEM),
        scratch_shapes=[
            vm((2, 1, 512), F32), vm((1, 1024), F32), vm((1024, 1024), BF), vm((512, 1024), BF),
            vm((8, 128), jnp.int32), vm((8, 128), jnp.int32), vm((1, 32), jnp.int32),
            vm((1, 128), jnp.int32), vm((1, 128), jnp.int32), vm((4, 32), jnp.int32), vm((8, 128), F32),
            vm((3, 2, 128, 1024), BF), vm((3, 2, 128, 512), BF), vm((2, 1024, 256), BF),
            vm((4, 2, 128, 512), BF), vm((2, 128, 512), BF),
            vm((2, 4, 32, 256), BF), vm((4, 2, 32, 256), BF),
            vm((4, 2, 256, 128), BF), vm((4, 2, 128, 256), BF),
            vm((8, 128), F32), vm((4, 8, 128), F32),
            vm((2, 2, 4, 3, 32, 512), BF), vm((2, 4, 2, 32, 512), BF),
            vm((2, 4, 2, 3, 32, 512), BF), vm((2, 4, 2, 32, 512), BF),
            vm((2, 4, 2, 4, 32, 512), BF), vm((4, 2, 2, 4, 32, 512), BF),
            vm((4, 2, 128, 512), BF), vm((2, 4, 128, 512), BF),
            dma((14,)), dma((5,)),
            dma((3,)), dma((2,)),
            dma((5,)), dma((3, 2)), dma((5,)), dma((3, 2)),
            dma((7,)), dma((4, 2)),
            dma((2,)), dma((2,)), dma((4,)), dma((4,)),
            dma((3, 7)), dma((3, 7)), dma((2, 7)), dma((2, 7)), dma((7,)), dma((7,)),
        ],
        compiler_params=pltpu.CompilerParams(
            collective_id=0, has_side_effects=True, vmem_limit_bytes=67_000_000
        ),
        cost_estimate=pl.CostEstimate(flops=5_000_000_000, bytes_accessed=5_000_000, transcendentals=600_000),
        name="moe_layer",
    )(
        attention, residual, out_proj, pre_gain.reshape(2, 1, 512), post_gain.reshape(1, -1),
        slot_gate_up[0], slot_down[0], expert_ids.T, copy_choice.T, placement.reshape(1, -1),
        request_age.reshape(1, -1), decode_flag.reshape(1, -1), capacity, route_weight.T,
    )


def solution(mesh):
    rows = P(("grp", "ep"), None)
    placed = (
        rows, rows, P(None, "grp"), P(), P(), P("ep", None, None), P("ep", None, None), rows, rows, P(),
        P(("grp", "ep")), P(("grp", "ep")), P(), rows,
    )
    return jax.shard_map(on_device, mesh=mesh, in_specs=placed, out_specs=rows, check_vma=False)
```

time: 72.1 us -> 61.9 us (0.86)
  Pallas kernels: 70.3 us -> 60 us
    pallas_call x1, Pallas kernels: 70.3 us -> 60 us  [on_device(): pl.pallas_call(kernel, out_shape=jax.ShapeDtypeStruct((128, 1024), BF), i...]
where the time goes in v2:
time: 61.9 us; the launch traced here: 61.7 us
  Pallas kernels  60 us (97%)
  local copies, waits for them, and re-layouts  1.67 us (3%)
    pallas_call x1, Pallas kernels, on_device(): pl.pallas_call(kernel, out_shape=jax.ShapeDtypeStruct((128, 1024), BF), i...  60 us
    unnamed x1, local copies, waits for them, and re-layouts  1.67 us

profile of v2, /device:TPU:1, one launch (start us, length us, event | category | flops | bytes accessed | tf_op | source)
XLA Modules:
  0.0 61.7 jit_solution(2106695600500011597)
XLA Ops:
  0.0 60.0 %moe_layer.1 = bf16[128,1024]{1,0:T(8,128)(2,1)} custom-call(bf16[128,1024]{1,0:T(8,128)(2,1)} %att_h.1, bf16[128,1024]{1,0:T(8,128)(2,1)} %res_h.1, bf16[1024,256]{1,0:T(8,128)(2,1)} %wo_h.1, f32[2,1,512]{2,1,0:T(1,128)} %bitcast.12, f32[1,1024]{1,0:T(1,128)} %bitcast.13, bf16[1024,1024]{1,0:T(8,128)(2,1)} %bitcast.10, bf16[512,1024]{1,0:T(8,128)(2,1)} %bitcast.11, ...), custom_call_target="tpu_custom_call" | custom-call | flops 5000000000 | bytes 5000000 | tf_op jit(solution)/shard_map/moe_layer/pallas_call | solution.py:339
  60.1 1.7 %copy.16 = bf16[128,1024]{1,0:T(8,128)(2,1)} copy(bf16[128,1024]{1,0:T(8,128)(2,1)} %moe_layer.1) | data formatting | bytes 524288

commit v3 on v2

v3 whole, which is shorter than its diff:
```python
import jax
import jax.numpy as jnp
from jax import lax
from jax.experimental import pallas as pl
from jax.experimental.pallas import tpu as pltpu
from jax.sharding import PartitionSpec as P

MESH = pl.DeviceIdType.MESH
BF = jnp.bfloat16
F32 = jnp.float32
DIST = (0, 1, 3, 2)


def dot(a, b):
    return jnp.dot(a, b, preferred_element_type=F32)


def kernel(
    att_h, res_h, wo_h, pre_h, post_h, gu_h, dn_h, ids_h, cc_h, place_h, age_h, flag_h, cap_h, rw_h,
    out_ref,
    pre, post, gu, dn, ids, cc, place, age, flag, cap, rw,
    att, res, wmine, hall, hfin, mw_src, mw_all, sel, comb_w, ss_src, ss_rcv,
    comp, rec, ob, comb, part_src, part_rcv,
    in_sem, loc_sem, w_s, w_f, w_r, a_s, a_r, r_s, r_r, m_s, m_r, h_s, h_r, q_s, q_r, d_s, d_r, e_s, e_r, p_s, p_r,
):
    z = lax.axis_index("grp")
    e = lax.axis_index("ep")
    x, y, c = e >> 3, (e >> 1) & 3, e & 1
    other = 1 - c

    def dev(dx, dy, core):
        return (z, ((x + dx) & 3) * 8 + ((y + dy) & 3) * 2 + core)

    def first(d, core):
        return dev(d * other, d * c, core)

    def second(d, core):
        return dev(d * c, d * other, core)

    bar = pltpu.get_barrier_semaphore()
    up, down = ((z + 1) & 3, e), ((z + 3) & 3, e)
    greet = [up, down, dev(0, 0, other)]
    for d in (1, 2, 3):
        for core in (0, 1):
            greet += [dev(d, 0, core), dev(0, d, core)]
    for to in greet:
        pl.semaphore_signal(bar, inc=1, device_id=to, device_id_type=MESH)

    def half_of(half):
        return pl.ds(pl.multiple_of(half * 512, 512), 512)

    sends = []

    def remote(src, dst, ss, rs, to):
        cp = pltpu.make_async_remote_copy(
            src_ref=src, dst_ref=dst, send_sem=ss, recv_sem=rs, device_id=to, device_id_type=MESH
        )
        cp.start()
        sends.append(cp)

    def arrived(dst, rs):
        pltpu.make_async_remote_copy(
            src_ref=dst, dst_ref=dst, send_sem=rs, recv_sem=rs, device_id=dev(0, 0, other), device_id_type=MESH
        ).wait_recv()

    has_w = c == z >> 1
    mine = z & 1
    w_cp = []
    for i, (to, h) in enumerate(((up, 0), (down, 1), (up, 1), (down, 0))):
        w_cp.append(
            pltpu.make_async_remote_copy(
                src_ref=wo_h.at[h], dst_ref=wmine.at[mine, h], send_sem=w_s.at[i], recv_sem=w_r.at[mine, h],
                device_id=to, device_id_type=MESH,
            )
        )
    w_local = pltpu.make_async_copy(wo_h, wmine.at[mine], in_sem.at[13])
    turn = (z - 2 * c) & 3
    near = ((turn + 1) >> 1) & 1
    relays = []
    for t, q, h, to in ((0, 1, 1, down), (1, 0, 0, up), (2, 1, 0, up), (3, 0, 1, down)):
        relays.append(
            (
                t,
                pltpu.make_async_remote_copy(
                    src_ref=wmine.at[q, h], dst_ref=wmine.at[q, h], send_sem=w_f.at[0], recv_sem=w_r.at[q, h],
                    device_id=to, device_id_type=MESH,
                ),
            )
        )
    pl.semaphore_wait(bar, len(greet))

    @pl.when(has_w)
    def _():
        for cp in w_cp:
            cp.start()
        w_local.start()

    k = 0
    for p in (1, 2):
        d = DIST[p]
        for half, to in ((0, dev(d, 0, 0)), (1, dev(0, d, 1))):
            remote(att_h, att.at[p, c], a_s.at[k], a_r.at[p, c], to)
            remote(res_h.at[:, half * 512 : half * 512 + 512], res.at[p, c], r_s.at[k], r_r.at[p, c], to)
            k += 1
    remote(att_h, att.at[0, c], a_s.at[k], a_r.at[0, c], dev(0, 0, other))
    remote(res_h.at[:, half_of(other)], res.at[0, c], r_s.at[k], r_r.at[0, c], dev(0, 0, other))

    loads = []
    for i, (src, dst) in enumerate(
        (
            (ids_h, ids), (cc_h, cc), (place_h, place), (age_h, age), (flag_h, flag), (cap_h, cap), (rw_h, rw),
            (att_h, att.at[0, c]), (res_h.at[:, half_of(c)], res.at[0, c]), (pre_h, pre), (post_h, post),
            (gu_h, gu), (dn_h, dn),
        )
    ):
        cp = pltpu.make_async_copy(src, dst, in_sem.at[i])
        cp.start()
        loads.append(cp)

    for cp in loads[:7]:
        cp.wait()
    row = lax.broadcasted_iota(jnp.int32, (128, 128), 0)
    lane = lax.broadcasted_iota(jnp.int32, (128, 128), 1)
    eye = row == lane
    pr_row = (flag[...] * 1048576 + age[...]).astype(F32)
    pr_col = jnp.sum(jnp.where(eye, pr_row, 0.0), axis=1, keepdims=True)
    ahead = jnp.where((pr_col > pr_row) | ((pr_col == pr_row) & (row < lane)), 1.0, 0.0)
    t = lax.broadcasted_iota(jnp.int32, (128, 32), 0)
    slot_lane = lax.broadcasted_iota(jnp.int32, (128, 32), 1)
    copy_of = t % 4
    px, py = t // 32, (t // 4) % 4
    dx = jnp.where(px < 2, px, 5 - px)
    dy = jnp.where(py < 2, py, 5 - py)
    slot = (((x + dx) % 4) * 4 + (y + dy) % 4) * 2 + (t // 16) % 2
    here = slot_lane == slot
    expert = jnp.sum(jnp.where(here, place[...].astype(F32), 0.0), axis=1, keepdims=True)
    code_col = expert * 4.0 + copy_of[:, :1].astype(F32)
    capf = cap[...].astype(F32)
    cap_sel = jnp.zeros((128, 32), F32)
    for g in range(4):
        cap_sel = jnp.where(here & (copy_of == g), capf[g : g + 1, :], cap_sel)
    cap_col = jnp.sum(cap_sel, axis=1, keepdims=True)
    code = (ids[...] * 4 + cc[...]).astype(F32)
    hits = jnp.zeros((128, 128), F32)
    weight = jnp.zeros((128, 128), F32)
    for i in range(8):
        same = code_col == code[i : i + 1, :]
        hits = jnp.where(same, 1.0, hits)
        weight = jnp.where(same, rw[i : i + 1, :], weight)
    counts = dot(hits.astype(BF), ahead.astype(BF))
    place_in = jnp.where((hits > 0.5) & (counts < cap_col), counts, 99.0)
    pw = jnp.concatenate([place_in, weight], axis=1)
    for p in range(4):
        mw_src[0, p] = pw[p * 32 : p * 32 + 32].astype(BF)
        blocks = []
        for core in range(2):
            for q in range(4):
                lo = q * 32 + core * 16 + p * 4
                blocks.append(pw[lo : lo + 4])
        mw_src[1, p] = jnp.concatenate(blocks, axis=0).astype(BF)
    k = 0
    for p in (1, 2, 3):
        d = DIST[p]
        for half, to in ((0, dev(d, 0, 0)), (1, dev(0, d, 1))):
            remote(mw_src.at[half, p], mw_all.at[p, c], m_s.at[k], m_r.at[p, c], to)
            k += 1
    remote(mw_src.at[other, 0], mw_all.at[0, c], m_s.at[k], m_r.at[0, c], dev(0, 0, other))
    mw_all[0, c] = mw_src[c, 0]

    for t, cp in relays:

        @pl.when(turn == t)
        def _():
            cp.wait_recv()
            cp.start()

    grow = jnp.where(
        lax.broadcasted_iota(jnp.int32, (256, 32), 0) // 8 == lax.broadcasted_iota(jnp.int32, (256, 32), 1), 1.0, 0.0
    ).astype(BF)
    p_row = (lax.broadcasted_iota(jnp.int32, (256, 128), 0) % 8).astype(F32)
    p_lane = (lax.broadcasted_iota(jnp.int32, (128, 256), 1) % 8).astype(F32)
    arrived(mw_all.at[0, other], m_r.at[0, other])
    for p in range(4):
        for core in (0, 1):
            if p:
                arrived(mw_all.at[p, core], m_r.at[p, core])
            both = mw_all[p, core]
            sel[p, core] = jnp.where(dot(grow, both[:, :128]) == p_row, 1.0, 0.0).astype(BF)
            wide = lax.dot_general(both, grow, (((0,), (1,)), ((), ())), preferred_element_type=F32)
            comb_w[p, core] = jnp.where(wide[:128] == p_lane, wide[128:], 0.0).astype(BF)

    def quarter_in(q):
        @pl.when(has_w & (mine == q))
        def _():
            w_local.wait()

        for h in (0, 1):
            relayed = ((0, 1, 1), (1, 0, 0), (2, 1, 0), (3, 0, 1))
            done = [t for t, rq, rh in relayed if rq == q and rh == h]
            waits = ~(has_w & (mine == q))
            for t in done:
                waits = waits & (turn != t)

            @pl.when(waits)
            def _():
                arrived(wmine.at[q, h], w_r.at[q, h])

    def project(p, q):
        rows = att[p].reshape(256, 1024)
        part = dot(rows, wmine[q].reshape(1024, 256)).reshape(2, 128, 256)
        cols = pl.ds(pl.multiple_of(q * 256, 256), 256)
        hall[p, :, :, cols] = (res[p, :, :, cols].astype(F32) + part).astype(BF)

    def squares(p, core):
        wide = hall[p, core].astype(F32)
        return jnp.sum(wide * wide, axis=1, keepdims=True)

    for cp in loads[7:]:
        cp.wait()
    arrived(att.at[0, other], a_r.at[0, other])
    arrived(res.at[0, other], r_r.at[0, other])
    for p in (1, 2):
        for core in (0, 1):
            arrived(att.at[p, core], a_r.at[p, core])
            arrived(res.at[p, core], r_r.at[p, core])
    for q in (0, 1):

        @pl.when(near == q)
        def _():
            quarter_in(q)

    for p in range(3):
        project(p, near)
    for q in (0, 1):

        @pl.when(near != q)
        def _():
            quarter_in(q)

    project(0, 1 - near)
    own_ss = {}
    for core in (0, 1):
        own_ss[0, core] = squares(0, core)
        ss_src[core : core + 1, :] = jnp.sum(jnp.where(eye, own_ss[0, core], 0.0), axis=0, keepdims=True)
    for p in (1, 2, 3):
        remote(ss_src, ss_rcv.at[p], q_s.at[p], q_r.at[p], second(DIST[p], other))
    remote(ss_src, ss_rcv.at[0], q_s.at[0], q_r.at[0], dev(0, 0, other))
    project(1, 1 - near)
    remote(hall.at[1, 0], hall.at[3, 0], h_s.at[0], h_r.at[0], first(1, c))
    project(2, 1 - near)
    remote(hall.at[2, 1], hall.at[3, 1], h_s.at[1], h_r.at[1], first(3, c))
    for p in (1, 2):
        for core in (0, 1):
            own_ss[p, core] = squares(p, core)
    gain = pre[c]

    def compact(p, core):
        own = own_ss[p, core]
        total = own + jnp.sum(jnp.where(eye, ss_rcv[p, core : core + 1, :], 0.0), axis=1, keepdims=True)
        scale = lax.rsqrt(total * (1.0 / 1024.0) + 1e-06)
        normed = (hall[p, core].astype(F32) * scale * gain).astype(BF)
        return dot(sel[p, core], normed).astype(BF).reshape(2, 4, 32, 512)

    local = []

    def part_of(kind):
        return ((0, pl.ds(0, 3)), (0, 3), (1,))[kind]

    def spread(kind):
        for p in (3, 1, 2):
            for core in (0, 1):
                remote(
                    comp.at[(core, p) + part_of(kind)], rec.at[(c, p) + part_of(kind)],
                    d_s.at[kind, core * 3 + p - 1], d_r.at[kind, c * 3 + p - 1], second(DIST[p], core),
                )
        remote(
            comp.at[(other, 0) + part_of(kind)], rec.at[(c, 0) + part_of(kind)], d_s.at[kind, 6], d_r.at[kind, 6],
            dev(0, 0, other),
        )
        cp = pltpu.make_async_copy(
            comp.at[(c, 0) + part_of(kind)], rec.at[(c, 0) + part_of(kind)], loc_sem.at[kind]
        )
        cp.start()
        local.append(cp)

    for p in range(3):
        arrived(ss_rcv.at[p], q_r.at[p])
        comp[:, :, 0, p] = compact(p, 0)
    spread(0)
    arrived(ss_rcv.at[3], q_r.at[3])
    for core in (0, 1):
        arrived(hall.at[3, core], h_r.at[core])
        own_ss[3, core] = squares(3, core)
    comp[:, :, 0, 3] = compact(3, 0)

    spread(1)
    for p in range(4):
        comp[:, :, 1, p] = compact(p, 1)
    spread(2)
    remote(hall.at[0, other], hfin.at[c], h_s.at[2], h_r.at[2], dev(0, 0, other))
    hfin[c] = hall[0, c]

    def places_in(kind):
        for half in (0, 1):
            for p in (1, 2, 3):
                arrived(rec.at[(half, p) + part_of(kind)], d_r.at[kind, half * 3 + p - 1])
        arrived(rec.at[(other, 0) + part_of(kind)], d_r.at[kind, 6])
        local[kind].wait()

    def back_part(kind):
        return ((0,), (1, pl.ds(1, 3)), (1, 0))[kind]

    back = []

    def give_back(kind, half, p):
        d = 4 - DIST[p]
        remote(
            ob.at[(half, p) + back_part(kind)], comb.at[(p, c) + back_part(kind)], e_s.at[kind, half * 3 + p - 1],
            e_r.at[kind, c * 3 + p - 1], dev(0, d, 0) if half == 0 else dev(d, 0, 1),
        )

    def give_chip(kind):
        remote(
            ob.at[(other, 0) + back_part(kind)], comb.at[(0, c) + back_part(kind)], e_s.at[kind, 6], e_r.at[kind, 6],
            dev(0, 0, other),
        )
        cp = pltpu.make_async_copy(
            ob.at[(c, 0) + back_part(kind)], comb.at[(0, c) + back_part(kind)], loc_sem.at[3 + kind]
        )
        cp.start()
        back.append(cp)

    for rows_of in (0, 1):
        if rows_of == 0:
            places_in(0)
            places_in(1)
        else:
            places_in(2)

        for pair in (0, 1):
            blocks = [(qy, qx) for qy in (2 * pair, 2 * pair + 1) for qx in range(4)]
            xa = jnp.concatenate([rec[0, qy, rows_of, qx] for qy, qx in blocks], axis=0)
            xb = jnp.concatenate([rec[1, qx, rows_of, qy] for qy, qx in blocks], axis=0)
            gate = dot(xa, gu[:512, :512]) + dot(xb, gu[512:, :512])
            raised = dot(xa, gu[:512, 512:]) + dot(xb, gu[512:, 512:])
            inner = (gate / (1.0 + jnp.exp(-gate)) * raised).astype(BF)
            made = dot(inner, dn[...]).astype(BF)
            for i, (qy, qx) in enumerate(blocks):
                ob[0, qy, rows_of, qx] = made[i * 32 : i * 32 + 32, :512]
                ob[1, qx, rows_of, qy] = made[i * 32 : i * 32 + 32, 512:]
            if pair == 0:
                give_back(rows_of, 0, 1)
            else:
                for half, p in ((0, 3), (1, 3), (1, 1), (0, 2), (1, 2)):
                    give_back(rows_of, half, p)
        give_chip(rows_of)
    for p in (3, 1, 2):
        for half in (0, 1):
            give_back(2, half, p)
    give_chip(2)

    def results_in(kind):
        for core in (0, 1):
            for p in (1, 2, 3):
                arrived(comb.at[(p, core) + back_part(kind)], e_r.at[kind, core * 3 + p - 1])
        arrived(comb.at[(0, other) + back_part(kind)], e_r.at[kind, 6])
        back[kind].wait()

    def weigh(p, rows_of):
        rows = jnp.concatenate([comb[q, core, rows_of, p] for core in (0, 1) for q in range(4)], axis=0)
        part_src[p, rows_of] = dot(comb_w[p, rows_of], rows).astype(BF)

    for rows_of in (0, 1):
        results_in(rows_of)
        for p in (3, 1, 2):
            weigh(p, rows_of)
            remote(
                part_src.at[p, rows_of], part_rcv.at[c, p], p_s.at[rows_of * 3 + p - 1], p_r.at[c * 3 + p - 1],
                first(4 - DIST[p], rows_of),
            )
    weigh(0, 0)
    results_in(2)
    weigh(0, 1)
    remote(part_src.at[0, other], part_rcv.at[c, 0], p_s.at[6], p_r.at[6], dev(0, 0, other))
    part_rcv[c, 0] = part_src[0, c]
    arrived(hfin.at[other], h_r.at[2])
    arrived(part_rcv.at[other, 0], p_r.at[6])
    values = []
    total = jnp.zeros((128, 1), F32)
    for half in (0, 1):
        v = hfin[half].astype(F32) + part_rcv[half, 0].astype(F32)
        for p in (1, 2, 3):
            arrived(part_rcv.at[half, p], p_r.at[half * 3 + p - 1])
            v = v + part_rcv[half, p].astype(F32)
        total = total + jnp.sum(v * v, axis=1, keepdims=True)
        values.append(v)
    scale = lax.rsqrt(total * (1.0 / 1024.0) + 1e-06)
    for half in (0, 1):
        cols = slice(half * 512, half * 512 + 512)
        out_ref[:, cols] = (values[half] * scale * post[:, cols]).astype(BF)
    for cp in sends:
        cp.wait_send()

    @pl.when(has_w)
    def _():
        for cp in w_cp:
            cp.wait_send()

    relays[0][1].wait_send()


def on_device(
    attention, residual, out_proj, pre_gain, post_gain, slot_gate_up, slot_down, expert_ids, copy_choice,
    placement, request_age, decode_flag, capacity, route_weight,
):
    dma = pltpu.SemaphoreType.DMA
    vm = pltpu.VMEM
    done = pl.pallas_call(
        kernel,
        out_shape=jax.ShapeDtypeStruct((128, 1024), BF),
        in_specs=[pl.BlockSpec(memory_space=pl.ANY)] * 14,
        out_specs=pl.BlockSpec(memory_space=pltpu.VMEM),
        scratch_shapes=[
            vm((2, 1, 512), F32), vm((1, 1024), F32), vm((1024, 1024), BF), vm((512, 1024), BF),
            vm((8, 128), jnp.int32), vm((8, 128), jnp.int32), vm((1, 32), jnp.int32),
            vm((1, 128), jnp.int32), vm((1, 128), jnp.int32), vm((4, 32), jnp.int32), vm((8, 128), F32),
            vm((3, 2, 128, 1024), BF), vm((3, 2, 128, 512), BF), vm((2, 2, 512, 256), BF),
            vm((4, 2, 128, 512), BF), vm((2, 128, 512), BF),
            vm((2, 4, 32, 256), BF), vm((4, 2, 32, 256), BF),
            vm((4, 2, 256, 128), BF), vm((4, 2, 128, 256), BF),
            vm((8, 128), F32), vm((4, 8, 128), F32),
            vm((2, 4, 2, 4, 32, 512), BF), vm((2, 4, 2, 4, 32, 512), BF),
            vm((2, 4, 2, 4, 32, 512), BF), vm((4, 2, 2, 4, 32, 512), BF),
            vm((4, 2, 128, 512), BF), vm((2, 4, 128, 512), BF),
            dma((14,)), dma((6,)),
            dma((4,)), dma((1,)), dma((2, 2)),
            dma((5,)), dma((3, 2)), dma((5,)), dma((3, 2)),
            dma((7,)), dma((4, 2)),
            dma((3,)), dma((3,)), dma((4,)), dma((4,)),
            dma((3, 7)), dma((3, 7)), dma((3, 7)), dma((3, 7)), dma((7,)), dma((7,)),
        ],
        compiler_params=pltpu.CompilerParams(
            collective_id=0, has_side_effects=True, vmem_limit_bytes=67_000_000
        ),
        cost_estimate=pl.CostEstimate(flops=5_000_000_000, bytes_accessed=5_000_000, transcendentals=600_000),
        name="moe_layer",
    )(
        attention, residual, out_proj.reshape(2, 512, 256), pre_gain.reshape(2, 1, 512), post_gain.reshape(1, -1),
        slot_gate_up[0], slot_down[0], expert_ids.T, copy_choice.T, placement.reshape(1, -1),
        request_age.reshape(1, -1), decode_flag.reshape(1, -1), capacity, route_weight.T,
    )
    return done


def solution(mesh):
    rows = P(("grp", "ep"), None)
    placed = (
        rows, rows, P(None, "grp"), P(), P(), P("ep", None, None), P("ep", None, None), rows, rows, P(),
        P(("grp", "ep")), P(("grp", "ep")), P(), rows,
    )
    return jax.shard_map(on_device, mesh=mesh, in_specs=placed, out_specs=rows, check_vma=False)
```

time: 61.9 us -> 59.7 us (0.964)
  Pallas kernels: 60 us -> 57.9 us
    pallas_call x1, Pallas kernels: 60 us -> 57.9 us  [on_device(): pl.pallas_call(kernel, out_shape=jax.ShapeDtypeStruct((128, 1024), BF), i...]
where the time goes in v3:
time: 59.7 us; the launch traced here: 59.6 us
  Pallas kernels  57.9 us (97%)
  local copies, waits for them, and re-layouts  1.67 us (3%)
    pallas_call x1, Pallas kernels, on_device(): pl.pallas_call(kernel, out_shape=jax.ShapeDtypeStruct((128, 1024), BF), i...  57.9 us
    unnamed x1, local copies, waits for them, and re-layouts  1.67 us

profile of v3, /device:TPU:1, one launch (start us, length us, event | category | flops | bytes accessed | tf_op | source)
XLA Modules:
  0.0 59.6 jit_solution(14218981913801050036)
XLA Ops:
  0.0 57.9 %moe_layer.1 = bf16[128,1024]{1,0:T(8,128)(2,1)} custom-call(bf16[128,1024]{1,0:T(8,128)(2,1)} %att_h.1, bf16[128,1024]{1,0:T(8,128)(2,1)} %res_h.1, bf16[2,512,256]{2,1,0:T(8,128)(2,1)} %bitcast.13, f32[2,1,512]{2,1,0:T(1,128)} %bitcast.14, f32[1,1024]{1,0:T(1,128)} %bitcast.15, bf16[1024,1024]{1,0:T(8,128)(2,1)} %bitcast.11, bf16[512,1024]{1,0:T(8,128)(2,1)} %bitcast.12, ...), custom_call_target="tpu_custom_call" | custom-call | flops 5000000000 | bytes 5000000 | tf_op jit(solution)/shard_map/moe_layer/pallas_call | solution.py:418
  57.9 1.7 %copy.16 = bf16[128,1024]{1,0:T(8,128)(2,1)} copy(bf16[128,1024]{1,0:T(8,128)(2,1)} %moe_layer.1) | data formatting | bytes 524288

commit v4 on v3

--- a/solution.py
+++ b/solution.py
@@ -9,6 +9,7 @@
 BF = jnp.bfloat16
 F32 = jnp.float32
 DIST = (0, 1, 3, 2)
+ONE, TWO = 1, 0
 
 
 def dot(a, b):
@@ -264,7 +265,7 @@
     local = []
 
     def part_of(kind):
-        return ((0, pl.ds(0, 3)), (0, 3), (1,))[kind]
+        return ((ONE, pl.ds(0, 3)), (ONE, 3), (TWO,))[kind]
 
     def spread(kind):
         for p in (3, 1, 2):
@@ -285,17 +286,17 @@
 
     for p in range(3):
         arrived(ss_rcv.at[p], q_r.at[p])
-        comp[:, :, 0, p] = compact(p, 0)
+        comp[:, :, ONE, p] = compact(p, ONE)
     spread(0)
     arrived(ss_rcv.at[3], q_r.at[3])
     for core in (0, 1):
         arrived(hall.at[3, core], h_r.at[core])
         own_ss[3, core] = squares(3, core)
-    comp[:, :, 0, 3] = compact(3, 0)
+    comp[:, :, ONE, 3] = compact(3, ONE)
 
     spread(1)
     for p in range(4):
-        comp[:, :, 1, p] = compact(p, 1)
+        comp[:, :, TWO, p] = compact(p, TWO)
     spread(2)
     remote(hall.at[0, other], hfin.at[c], h_s.at[2], h_r.at[2], dev(0, 0, other))
     hfin[c] = hall[0, c]
@@ -308,7 +309,7 @@
         local[kind].wait()
 
     def back_part(kind):
-        return ((0,), (1, pl.ds(1, 3)), (1, 0))[kind]
+        return ((ONE,), (TWO, pl.ds(1, 3)), (TWO, 0))[kind]
 
     back = []
 
@@ -330,8 +331,8 @@
         cp.start()
         back.append(cp)
 
-    for rows_of in (0, 1):
-        if rows_of == 0:
+    for step, rows_of in ((0, ONE), (1, TWO)):
+        if step == 0:
             places_in(0)
             places_in(1)
         else:
@@ -349,15 +350,17 @@
                 ob[0, qy, rows_of, qx] = made[i * 32 : i * 32 + 32, :512]
                 ob[1, qx, rows_of, qy] = made[i * 32 : i * 32 + 32, 512:]
             if pair == 0:
-                give_back(rows_of, 0, 1)
+                give_back(step, 0, 1)
             else:
                 for half, p in ((0, 3), (1, 3), (1, 1), (0, 2), (1, 2)):
-                    give_back(rows_of, half, p)
-        give_chip(rows_of)
+                    give_back(step, half, p)
+        give_chip(step)
     for p in (3, 1, 2):
         for half in (0, 1):
             give_back(2, half, p)
     give_chip(2)
+
+    before = len(sends)
 
     def results_in(kind):
         for core in (0, 1):
@@ -370,19 +373,29 @@
         rows = jnp.concatenate([comb[q, core, rows_of, p] for core in (0, 1) for q in range(4)], axis=0)
         part_src[p, rows_of] = dot(comb_w[p, rows_of], rows).astype(BF)
 
-    for rows_of in (0, 1):
-        results_in(rows_of)
+    for step, rows_of in ((0, ONE), (1, TWO)):
+        results_in(step)
         for p in (3, 1, 2):
             weigh(p, rows_of)
             remote(
                 part_src.at[p, rows_of], part_rcv.at[c, p], p_s.at[rows_of * 3 + p - 1], p_r.at[c * 3 + p - 1],
                 first(4 - DIST[p], rows_of),
             )
-    weigh(0, 0)
+    weigh(0, ONE)
     results_in(2)
-    weigh(0, 1)
+    weigh(0, TWO)
     remote(part_src.at[0, other], part_rcv.at[c, 0], p_s.at[6], p_r.at[6], dev(0, 0, other))
     part_rcv[c, 0] = part_src[0, c]
+    for cp in sends[:before]:
+        cp.wait_send()
+
+    @pl.when(has_w)
+    def _():
+        for cp in w_cp:
+            cp.wait_send()
+
+    relays[0][1].wait_send()
+
     arrived(hfin.at[other], h_r.at[2])
     arrived(part_rcv.at[other, 0], p_r.at[6])
     values = []
@@ -398,15 +411,8 @@
     for half in (0, 1):
         cols = slice(half * 512, half * 512 + 512)
         out_ref[:, cols] = (values[half] * scale * post[:, cols]).astype(BF)
-    for cp in sends:
+    for cp in sends[before:]:
         cp.wait_send()
-
-    @pl.when(has_w)
-    def _():
-        for cp in w_cp:
-            cp.wait_send()
-
-    relays[0][1].wait_send()
 
 
 def on_device(

time: 59.7 us -> 58.9 us (0.987); the launches traced: 59.6 us -> 57.9 us
  Pallas kernels: 57.9 us -> 56.3 us
    pallas_call x1, Pallas kernels: 57.9 us -> 56.3 us  [on_device(): pl.pallas_call(kernel, out_shape=jax.ShapeDtypeStruct((128, 1024), BF), i...]
where the time goes in v4:
time: 58.9 us; the launch traced here: 57.9 us
  Pallas kernels  56.3 us (96%)
  local copies, waits for them, and re-layouts  1.67 us (3%)
    pallas_call x1, Pallas kernels, on_device(): pl.pallas_call(kernel, out_shape=jax.ShapeDtypeStruct((128, 1024), BF), i...  56.3 us
    unnamed x1, local copies, waits for them, and re-layouts  1.67 us

profile of v4, /device:TPU:1, one launch (start us, length us, event | category | flops | bytes accessed | tf_op | source)
XLA Modules:
  0.0 57.9 jit_solution(5961326685445978549)
XLA Ops:
  0.0 56.3 %moe_layer.1 = bf16[128,1024]{1,0:T(8,128)(2,1)} custom-call(bf16[128,1024]{1,0:T(8,128)(2,1)} %att_h.1, bf16[128,1024]{1,0:T(8,128)(2,1)} %res_h.1, bf16[2,512,256]{2,1,0:T(8,128)(2,1)} %bitcast.13, f32[2,1,512]{2,1,0:T(1,128)} %bitcast.14, f32[1,1024]{1,0:T(1,128)} %bitcast.15, bf16[1024,1024]{1,0:T(8,128)(2,1)} %bitcast.11, bf16[512,1024]{1,0:T(8,128)(2,1)} %bitcast.12, ...), custom_call_target="tpu_custom_call" | custom-call | flops 5000000000 | bytes 5000000 | tf_op jit(solution)/shard_map/moe_layer/pallas_call | solution.py:424
  56.3 1.7 %copy.16 = bf16[128,1024]{1,0:T(8,128)(2,1)} copy(bf16[128,1024]{1,0:T(8,128)(2,1)} %moe_layer.1) | data formatting | bytes 524288

commit v5 on v4

--- a/solution.py
+++ b/solution.py
@@ -42,8 +42,7 @@
     up, down = ((z + 1) & 3, e), ((z + 3) & 3, e)
     greet = [up, down, dev(0, 0, other)]
     for d in (1, 2, 3):
-        for core in (0, 1):
-            greet += [dev(d, 0, core), dev(0, d, core)]
+        greet += [first(d, 0), first(d, 1), second(d, c)]
     for to in greet:
         pl.semaphore_signal(bar, inc=1, device_id=to, device_id_type=MESH)
 
@@ -338,7 +337,7 @@
         else:
             places_in(2)
 
-        for pair in (0, 1):
+        for pair in (1, 0):
             blocks = [(qy, qx) for qy in (2 * pair, 2 * pair + 1) for qx in range(4)]
             xa = jnp.concatenate([rec[0, qy, rows_of, qx] for qy, qx in blocks], axis=0)
             xb = jnp.concatenate([rec[1, qx, rows_of, qy] for qy, qx in blocks], axis=0)
@@ -349,11 +348,12 @@
             for i, (qy, qx) in enumerate(blocks):
                 ob[0, qy, rows_of, qx] = made[i * 32 : i * 32 + 32, :512]
                 ob[1, qx, rows_of, qy] = made[i * 32 : i * 32 + 32, 512:]
-            if pair == 0:
-                give_back(step, 0, 1)
+            if pair == 1:
+                early = ((0, 3), (0, 2))
             else:
-                for half, p in ((0, 3), (1, 3), (1, 1), (0, 2), (1, 2)):
-                    give_back(step, half, p)
+                early = ((1, 3), (1, 1), (0, 1), (1, 2))
+            for half, p in early:
+                give_back(step, half, p)
         give_chip(step)
     for p in (3, 1, 2):
         for half in (0, 1):

time: 58.9 us -> 59 us (level)
  no operation moved by 1% of the time
where the time goes in v5:
time: 59 us; the launch traced here: 58.1 us
  Pallas kernels  56.4 us (96%)
  local copies, waits for them, and re-layouts  1.67 us (3%)
    pallas_call x1, Pallas kernels, on_device(): pl.pallas_call(kernel, out_shape=jax.ShapeDtypeStruct((128, 1024), BF), i...  56.4 us
    unnamed x1, local copies, waits for them, and re-layouts  1.67 us

profile of v5, /device:TPU:1, one launch (start us, length us, event | category | flops | bytes accessed | tf_op | source)
XLA Modules:
  0.0 58.1 jit_solution(9553920199874087617)
XLA Ops:
  0.0 56.4 %moe_layer.1 = bf16[128,1024]{1,0:T(8,128)(2,1)} custom-call(bf16[128,1024]{1,0:T(8,128)(2,1)} %att_h.1, bf16[128,1024]{1,0:T(8,128)(2,1)} %res_h.1, bf16[2,512,256]{2,1,0:T(8,128)(2,1)} %bitcast.13, f32[2,1,512]{2,1,0:T(1,128)} %bitcast.14, f32[1,1024]{1,0:T(1,128)} %bitcast.15, bf16[1024,1024]{1,0:T(8,128)(2,1)} %bitcast.11, bf16[512,1024]{1,0:T(8,128)(2,1)} %bitcast.12, ...), custom_call_target="tpu_custom_call" | custom-call | flops 5000000000 | bytes 5000000 | tf_op jit(solution)/shard_map/moe_layer/pallas_call | solution.py:424
  56.4 1.7 %copy.16 = bf16[128,1024]{1,0:T(8,128)(2,1)} copy(bf16[128,1024]{1,0:T(8,128)(2,1)} %moe_layer.1) | data formatting | bytes 524288
